TPU v7x, 32 devices: a whole 2x2x4 slice. The times are simulated.
32 devices in a mesh: seq: 4 (over y, core), dp: 8 (over z, x).
Axes of the slice: x: 2, y: 2, z: 4, core: 2. Of those that a mesh axis runs over, the one named last changes fastest.
Arguments:
- tokens: bfloat16 [8, 2048, 1024], P('dp', 'seq'), may hold values from -6 to 6
- cotangent: bfloat16 [8, 2048, 1024], P('dp', 'seq'), may hold values from -6 to 6
- segments: int32 [8, 2048], P('dp'), may hold values from 0 to 2047, as said below
- routes: int32 [8, 2048, 8], P('dp', 'seq'), may hold values from 0 to 15, all different within a row; in each aligned block of 512 rows (0 to 511, 512 to 1023, ..., all dimensions but the last counted through in order) at most 320 rows name the same one
- w_qkv: bfloat16 [1024, 2048], P(None, ('seq', 'dp')), may hold values from -0.25 to 0.25
- w_out: bfloat16 [1024, 1024], P(None, ('seq', 'dp')), may hold values from -1 to 1
- norm_gains: bfloat16 [2, 1024], P(None, ('seq', 'dp')), may hold values from 0.5 to 1.5
- router: bfloat16 [16, 1024], P(None, ('seq', 'dp')), may hold values from -0.09375 to 0.09375
- w_gate_up: bfloat16 [16, 1024, 1024], P(None, None, ('seq', 'dp')), may hold values from -0.1875 to 0.1875
- w_down: bfloat16 [16, 512, 1024], P(None, None, ('seq', 'dp')), may hold values from -1.5 to 1.5
Outputs:
- mixed: bfloat16 [8, 2048, 1024], P('dp', 'seq')
- input_grad: float32 [8, 2048, 1024], P('dp', 'seq')
- grad_qkv: float32 [1024, 2048], P(None, ('seq', 'dp'))
- grad_out: float32 [1024, 1024], P(None, ('seq', 'dp'))
- grad_gains: float32 [2, 1024], P(None, ('seq', 'dp'))
- grad_router: float32 [16, 1024], P(None, ('seq', 'dp'))
- grad_gate_up: float32 [16, 1024, 1024], P(None, None, ('seq', 'dp'))
- grad_down: float32 [16, 512, 1024], P(None, None, ('seq', 'dp'))
Inputs may be any that keep to these rules, and one draw needn't show every extreme that they name: segments[b, i] is the index of the first token of the document holding token i; it never decreases along a sequence and starts at 0. `routes`: each token names 8 different experts; within each aligned block of 512 tokens of a sequence no expert is named by more than 320 tokens, and in some block one is named by exactly 320.
All inputs are finite; a program needn't handle non-finite values.
Results may differ from a plain program's by a relative error of at most 0.017.
The roundings to bfloat16 on the way count: a program that leaves them out, or rounds other values in their place, can miss the bound.
Values may be sent and summed in bfloat16 or wider, within the bound.
A program may use at most 384 MiB of HBM per device.

v0:
```python
import jax
import jax.numpy as jnp
from jax import lax
from jax.sharding import PartitionSpec as P

HEADS = 16
KV_HEADS = 8
HEAD_DIM = 64
FF = 512
TOP = 8
EXPERTS = 16
CAP = 320


NORM_EPSILON = 1e-06
ROPE_THETA = 10000.0


def rms_scale(tensor):
    return lax.rsqrt(jnp.mean(tensor * tensor, axis=-1, keepdims=True) + NORM_EPSILON)


def rotate(tensor, positions, direction):
    half_dim = tensor.shape[-1] // 2
    frequency = ROPE_THETA ** (-jnp.arange(half_dim, dtype=jnp.float32) / half_dim)
    angles = positions.astype(jnp.float32)[:, None] * frequency[None, :]
    cosine = jnp.cos(angles)[:, None, :]
    sine_part = direction * jnp.sin(angles)[:, None, :]
    first_half = tensor[..., :half_dim]
    second_half = tensor[..., half_dim:]
    return jnp.concatenate(
        [
            first_half * cosine - second_half * sine_part,
            second_half * cosine + first_half * sine_part,
        ],
        axis=-1,
    )


def route_tables(route_rows, expert_count, capacity):
    pair_count = route_rows.shape[0] * route_rows.shape[1]
    flat_routes = route_rows.reshape(pair_count)
    expert_hits = (
        flat_routes[:, None] == jnp.arange(expert_count, dtype=jnp.int32)[None, :]
    ).astype(jnp.int32)
    running = jnp.cumsum(expert_hits, axis=0, dtype=jnp.int32) - 1
    within = jnp.sum(running * expert_hits, axis=1, dtype=jnp.int32)
    slot_of_pair = flat_routes * capacity + within
    slot_table = jnp.full((expert_count * capacity,), pair_count, dtype=jnp.int32)
    slot_table = slot_table.at[slot_of_pair].set(jnp.arange(pair_count, dtype=jnp.int32))
    return (slot_of_pair, slot_table)


def per_device(
    tokens, cotangent, segments, routes, w_qkv, w_out, norm_gains, router, w_gate_up, w_down
):
    dense_full = (
        lax.all_gather(w_qkv, ("seq", "dp"), axis=1, tiled=True),
        lax.all_gather(w_out, ("seq", "dp"), axis=1, tiled=True),
        lax.all_gather(norm_gains, ("seq", "dp"), axis=1, tiled=True),
        lax.all_gather(router, ("seq", "dp"), axis=1, tiled=True),
    )
    expert_full = (
        lax.all_gather(w_gate_up, ("seq", "dp"), axis=2, tiled=True),
        lax.all_gather(w_down, ("seq", "dp"), axis=2, tiled=True),
    )
    qkv_proj, out_proj, gain_rows, router_proj = dense_full
    gate_up, down_proj = expert_full
    norm_gain = gain_rows.astype(jnp.float32)
    inputs = tokens[0].astype(jnp.float32)
    row_count = inputs.shape[0]
    feature_count = inputs.shape[1]
    length = segments.shape[1]
    score_scale = HEAD_DIM ** (-0.5)
    query_width = HEADS * HEAD_DIM
    key_width = KV_HEADS * HEAD_DIM
    group_size = HEADS // KV_HEADS
    row_start = lax.axis_index("seq") * row_count
    own_index = row_start + jnp.arange(row_count, dtype=jnp.int32)
    segment_row = segments[0]
    own_segment = lax.dynamic_slice_in_dim(segment_row, row_start, row_count)
    rotary = own_index - own_segment
    key_index = jnp.arange(length, dtype=jnp.int32)
    key_mask = (key_index[None, :] <= own_index[:, None]) & (
        segment_row[None, :] == own_segment[:, None]
    )
    first_scale = rms_scale(inputs)
    first_normed = inputs * first_scale
    first_hidden = (first_normed * norm_gain[0]).astype(jnp.bfloat16)
    projected = jnp.dot(first_hidden, qkv_proj, preferred_element_type=jnp.float32)
    queries = rotate(
        projected[:, :query_width].reshape(row_count, HEADS, HEAD_DIM), rotary, 1.0
    ).astype(jnp.bfloat16)
    key_rows = rotate(
        projected[:, query_width : query_width + key_width].reshape(row_count, KV_HEADS, HEAD_DIM),
        rotary,
        1.0,
    ).astype(jnp.bfloat16)
    value_rows = projected[:, query_width + key_width :].astype(jnp.bfloat16)
    outgoing = jnp.concatenate([key_rows.reshape(row_count, key_width), value_rows], axis=1)
    sequence_kv = lax.all_gather(outgoing, "seq", axis=0, tiled=True)
    keys_all = sequence_kv[:, :key_width].reshape(length, KV_HEADS, HEAD_DIM).transpose(1, 0, 2)
    values_all = sequence_kv[:, key_width:].reshape(length, KV_HEADS, HEAD_DIM).transpose(1, 0, 2)
    query_heads = queries.reshape(row_count, KV_HEADS, group_size, HEAD_DIM).transpose(1, 0, 2, 3)

    def head_scores(query_group, key_head):
        scores = (
            jnp.einsum("qgd,kd->gqk", query_group, key_head, preferred_element_type=jnp.float32)
            * score_scale
        )
        return jnp.where(key_mask[None], scores, -1e30)

    def forward_head(operands):
        query_group, key_head, value_head = operands
        scores = head_scores(query_group, key_head)
        row_peak = jnp.max(scores, axis=-1, keepdims=True)
        shifted = jnp.exp(scores - row_peak)
        row_total = jnp.sum(shifted, axis=-1, keepdims=True)
        softmax_weights = (shifted / row_total).astype(jnp.bfloat16)
        attended_head = jnp.einsum(
            "gqk,kd->qgd", softmax_weights, value_head, preferred_element_type=jnp.float32
        )
        return (attended_head.astype(jnp.bfloat16), (row_peak + jnp.log(row_total))[..., 0])

    attended_heads, log_totals = lax.map(forward_head, (query_heads, keys_all, values_all))
    attended = attended_heads.transpose(1, 0, 2, 3).reshape(row_count, query_width)
    residual = inputs + jnp.dot(attended, out_proj, preferred_element_type=jnp.float32)
    second_scale = rms_scale(residual)
    second_normed = residual * second_scale
    second_hidden = (second_normed * norm_gain[1]).astype(jnp.bfloat16)
    logits = lax.dot_general(
        second_hidden, router_proj, (((1,), (1,)), ((), ())), preferred_element_type=jnp.float32
    )
    route_rows = routes[0]
    matches = route_rows[:, :, None] == jnp.arange(EXPERTS, dtype=jnp.int32)[None, None, :]
    chosen = jnp.sum(jnp.where(matches, logits[:, None, :], 0.0), axis=-1)
    gate_values = jax.nn.softmax(chosen, axis=-1)
    slot_of_pair, slot_table = route_tables(route_rows, EXPERTS, CAP)
    token_of_slot = slot_table // TOP
    padded = jnp.concatenate([second_hidden, jnp.zeros((1, feature_count), jnp.bfloat16)], axis=0)
    expert_input = padded[token_of_slot].reshape(EXPERTS, CAP, feature_count)
    gate_up_out = jnp.einsum(
        "ecd,edf->ecf", expert_input, gate_up, preferred_element_type=jnp.float32
    )
    gate_part = gate_up_out[..., :FF]
    up_part = gate_up_out[..., FF:]
    silu_gate = jax.nn.silu(gate_part)
    swiglu_out = (silu_gate * up_part).astype(jnp.bfloat16)
    expert_out = jnp.einsum(
        "ecf,efd->ecd", swiglu_out, down_proj, preferred_element_type=jnp.float32
    )
    gate_flat = jnp.concatenate(
        [gate_values.reshape(row_count * TOP), jnp.zeros((1,), jnp.float32)]
    )
    slot_gates = gate_flat[slot_table].reshape(EXPERTS, CAP, 1)
    weighted = (expert_out * slot_gates).reshape(EXPERTS * CAP, feature_count)
    mixture = jax.ops.segment_sum(weighted, token_of_slot, num_segments=row_count + 1)[:row_count]
    mixed = (residual + mixture).astype(jnp.bfloat16)[None]
    back_dense = (
        lax.all_gather(w_qkv, ("seq", "dp"), axis=1, tiled=True),
        lax.all_gather(w_out, ("seq", "dp"), axis=1, tiled=True),
        lax.all_gather(norm_gains, ("seq", "dp"), axis=1, tiled=True),
        lax.all_gather(router, ("seq", "dp"), axis=1, tiled=True),
    )
    back_expert = (
        lax.all_gather(w_gate_up, ("seq", "dp"), axis=2, tiled=True),
        lax.all_gather(w_down, ("seq", "dp"), axis=2, tiled=True),
    )
    qkv_back, out_back, gain_back, router_back = back_dense
    gate_up_back, down_back = back_expert
    gain_again = gain_back.astype(jnp.float32)
    grad_output = cotangent[0].astype(jnp.float32)
    grad_padded = jnp.concatenate([grad_output, jnp.zeros((1, feature_count), jnp.float32)], axis=0)
    routed_grad = grad_padded[token_of_slot].reshape(EXPERTS, CAP, feature_count)
    grad_expert_out = (routed_grad * slot_gates).astype(jnp.bfloat16)
    slot_grad = jnp.sum(routed_grad * expert_out, axis=-1).reshape(EXPERTS * CAP)
    grad_gates = slot_grad[slot_of_pair].reshape(row_count, TOP)
    grad_swiglu = jnp.einsum(
        "ecd,efd->ecf", grad_expert_out, down_back, preferred_element_type=jnp.float32
    )
    grad_down_local = jnp.einsum(
        "ecf,ecd->efd", swiglu_out, grad_expert_out, preferred_element_type=jnp.float32
    )
    sigmoid_gate = jax.nn.sigmoid(gate_part)
    silu_slope = sigmoid_gate * (1.0 + gate_part * (1.0 - sigmoid_gate))
    grad_gate_up_out = jnp.concatenate(
        [grad_swiglu * up_part * silu_slope, grad_swiglu * silu_gate], axis=-1
    ).astype(jnp.bfloat16)
    grad_expert_in = jnp.einsum(
        "ecf,edf->ecd", grad_gate_up_out, gate_up_back, preferred_element_type=jnp.float32
    )
    grad_gate_up_local = jnp.einsum(
        "ecd,ecf->edf", expert_input, grad_gate_up_out, preferred_element_type=jnp.float32
    )
    grad_second = jax.ops.segment_sum(
        grad_expert_in.reshape(EXPERTS * CAP, feature_count),
        token_of_slot,
        num_segments=row_count + 1,
    )[:row_count]
    grad_chosen = gate_values * (
        grad_gates - jnp.sum(gate_values * grad_gates, axis=-1, keepdims=True)
    )
    grad_logits = jnp.sum(jnp.where(matches, grad_chosen[:, :, None], 0.0), axis=1).astype(
        jnp.bfloat16
    )
    grad_second = grad_second + jnp.dot(
        grad_logits, router_back, preferred_element_type=jnp.float32
    )
    grad_router_local = lax.dot_general(
        grad_logits, second_hidden, (((0,), (0,)), ((), ())), preferred_element_type=jnp.float32
    )
    gain_two = jnp.sum(grad_second * second_normed, axis=0)
    grad_normed_two = grad_second * gain_again[1]
    grad_residual = grad_output + second_scale * (
        grad_normed_two
        - second_normed * jnp.mean(grad_normed_two * second_normed, axis=-1, keepdims=True)
    )
    grad_branch = grad_residual.astype(jnp.bfloat16)
    grad_attended = lax.dot_general(
        grad_branch, out_back, (((1,), (1,)), ((), ())), preferred_element_type=jnp.float32
    ).astype(jnp.bfloat16)
    grad_out_local = lax.dot_general(
        attended, grad_branch, (((0,), (0,)), ((), ())), preferred_element_type=jnp.float32
    )
    grad_heads = grad_attended.reshape(row_count, KV_HEADS, group_size, HEAD_DIM).transpose(
        1, 0, 2, 3
    )

    def backward_head(operands):
        query_group, key_head, value_head, grad_group, log_total = operands
        scores = head_scores(query_group, key_head)
        softmax_full = jnp.exp(scores - log_total[..., None])
        grad_weights = jnp.einsum(
            "qgd,kd->gqk", grad_group, value_head, preferred_element_type=jnp.float32
        )
        row_delta = jnp.sum(softmax_full * grad_weights, axis=-1, keepdims=True)
        grad_scores = (softmax_full * (grad_weights - row_delta)).astype(jnp.bfloat16)
        grad_query = (
            jnp.einsum("gqk,kd->qgd", grad_scores, key_head, preferred_element_type=jnp.float32)
            * score_scale
        )
        grad_key = (
            jnp.einsum("gqk,qgd->kd", grad_scores, query_group, preferred_element_type=jnp.float32)
            * score_scale
        )
        grad_value = jnp.einsum(
            "gqk,qgd->kd",
            softmax_full.astype(jnp.bfloat16),
            grad_group,
            preferred_element_type=jnp.float32,
        )
        return (grad_query, grad_key, grad_value)

    query_grads, key_grads, value_grads = lax.map(
        backward_head, (query_heads, keys_all, values_all, grad_heads, log_totals)
    )
    key_terms = jnp.concatenate(
        [
            key_grads.transpose(1, 0, 2).reshape(length, key_width),
            value_grads.transpose(1, 0, 2).reshape(length, key_width),
        ],
        axis=1,
    )
    key_owned = lax.psum_scatter(
        key_terms.astype(jnp.bfloat16), "seq", scatter_dimension=0, tiled=True
    ).astype(jnp.float32)
    grad_query_rows = rotate(
        query_grads.transpose(1, 0, 2, 3).reshape(row_count, HEADS, HEAD_DIM), rotary, -1.0
    ).reshape(row_count, query_width)
    grad_key_rows = rotate(
        key_owned[:, :key_width].reshape(row_count, KV_HEADS, HEAD_DIM), rotary, -1.0
    ).reshape(row_count, key_width)
    grad_projected = jnp.concatenate(
        [grad_query_rows, grad_key_rows, key_owned[:, key_width:]], axis=1
    ).astype(jnp.bfloat16)
    grad_first = lax.dot_general(
        grad_projected, qkv_back, (((1,), (1,)), ((), ())), preferred_element_type=jnp.float32
    )
    grad_qkv_local = lax.dot_general(
        first_hidden, grad_projected, (((0,), (0,)), ((), ())), preferred_element_type=jnp.float32
    )
    gain_one = jnp.sum(grad_first * first_normed, axis=0)
    grad_normed_one = grad_first * gain_again[0]
    input_grad = grad_residual + first_scale * (
        grad_normed_one
        - first_normed * jnp.mean(grad_normed_one * first_normed, axis=-1, keepdims=True)
    )
    gain_grads = jnp.stack([gain_one, gain_two])
    dense_owned = (
        lax.psum_scatter(grad_qkv_local, ("seq", "dp"), scatter_dimension=1, tiled=True),
        lax.psum_scatter(grad_out_local, ("seq", "dp"), scatter_dimension=1, tiled=True),
        lax.psum_scatter(gain_grads, ("seq", "dp"), scatter_dimension=1, tiled=True),
        lax.psum_scatter(grad_router_local, ("seq", "dp"), scatter_dimension=1, tiled=True),
    )
    expert_owned = (
        lax.psum_scatter(grad_gate_up_local, ("seq", "dp"), scatter_dimension=2, tiled=True),
        lax.psum_scatter(grad_down_local, ("seq", "dp"), scatter_dimension=2, tiled=True),
    )
    return (
        mixed,
        input_grad[None],
        dense_owned[0],
        dense_owned[1],
        dense_owned[2],
        dense_owned[3],
        expert_owned[0],
        expert_owned[1],
    )


def solution(mesh):
    placed = (
        P("dp", "seq", None),
        P("dp", "seq", None),
        P("dp", None),
        P("dp", "seq", None),
        P(None, ("seq", "dp")),
        P(None, ("seq", "dp")),
        P(None, ("seq", "dp")),
        P(None, ("seq", "dp")),
        P(None, None, ("seq", "dp")),
        P(None, None, ("seq", "dp")),
    )
    return jax.shard_map(
        per_device,
        mesh=mesh,
        in_specs=placed,
        out_specs=(
            P("dp", "seq", None),
            P("dp", "seq", None),
            P(None, ("seq", "dp")),
            P(None, ("seq", "dp")),
            P(None, ("seq", "dp")),
            P(None, ("seq", "dp")),
            P(None, None, ("seq", "dp")),
            P(None, None, ("seq", "dp")),
        ),
        check_vma=False,
    )
```

profile of v0, /device:TPU:0, one launch (start us, length us, event | category | flops | bytes accessed | tf_op | source)
XLA Modules:
  0.0 3658.8 jit_solution(17789269875407110917)
XLA Ops:
  8.0 69.5 %all-gather = bf16[32,32,2]{1,2,0:T(2,128)(2,1)S(1)} all-gather(bf16[1,32,2]{1,2,0:T(2,128)(2,1)} %bitcast.332), channel_id=1, replica_groups=mesh['seq'=4,'dp'=8] {'seq','dp'}, dimensions={0}, use_global_device_ids=true | all-gather | bytes 4224 | tf_op jit(solution)/shard_map/all_gather | solution.py:60
  81.4 4.9 fusion.95
  94.7 4.6 reduce-window.6
  101.0 15.5 scatter_custom_fusion
  117.2 64.3 %all-gather.1 = bf16[32,32,16]{1,2,0:T(8,128)(2,1)S(1)} all-gather(bf16[1,32,16]{1,2,0:T(8,128)(2,1)S(1)} %bitcast.330), channel_id=1, replica_groups=mesh['seq'=4,'dp'=8] {'seq','dp'}, dimensions={0}, use_global_device_ids=true | all-gather | bytes 33792 | tf_op jit(solution)/shard_map/all_gather | solution.py:61
  184.0 23.1 gather_fusion.2
  221.7 75.3 %while.28 = (s32[]{:T(128)}, bf16[8,512,2,64]{1,3,2,0:T(8,128)(2,1)}, f32[8,2,512]{2,1,0:T(2,128)}, bf16[8,2048,64]{1,2,0:T(8,128)(2,1)}, bf16[8,2048,64]{1,2,0:...) while((s32[]{:T(128)}, ...), condition=%wide.region_4.5_spmd.clone, body=%wide.region_1.4_spmd.clone.sunk | while | flops 565246976 | bytes 30193776 | solution.py:125
  303.8 22.4 gather_fusion
  327.9 49.0 %all-gather.14.cloned.1.call-done = bf16[16,1024,1024]{1,2,0:T(8,128)(2,1)} async-done(((bf16[16,1024,32]{1,2,0:T(8,128)(2,1)}), bf16[16,1024,1024]{1,2,0:T(8,128)(2,1)}) %all-gather.14.cloned.1.call-update) | async-done | bytes 33554448 | tf_op jit(solution)/shard_map/all_gather | solution.py:64
  376.9 24.9 fusion.118
  401.8 12.0 multiply_convert_fusion.3
  413.8 80.3 %all-gather.16.cloned.1.call-done = bf16[16,512,1024]{1,2,0:T(8,128)(2,1)} async-done(((bf16[16,512,32]{1,2,0:T(8,128)(2,1)}), bf16[16,512,1024]{1,2,0:T(8,128)(2,1)}) %all-gather.16.cloned.1.call-update) | async-done | bytes 16777232 | tf_op jit(solution)/shard_map/all_gather | solution.py:65
  494.1 21.2 multiply_reduce_fusion
  515.4 23.0 gather_fusion.3
  539.1 28.7 gather_fusion.1
  567.8 26.8 multiply_convert_fusion.2
  594.6 28.0 fusion.68
  622.6 46.6 %scatter_custom_fusion.2 = f32[513,1024]{1,0:T(8,128)} fusion(s32[5120]{0:T(1024)} %get-tuple-element.227, f32[5120,1024]{1,0:T(8,128)} %bitcast.333, f32[]{:T(128)} %constant.63.clone.1), kind=kCustom, calls=%fused_computation.118 | custom fusion | flops 5242880 | bytes 2101760 | tf_op jit(solution)/shard_map/scatter-add | solution.py:195
  672.8 15.9 broadcast_multiply_fusion
  688.6 46.4 %scatter_custom_fusion.1 = f32[513,1024]{1,0:T(8,128)} fusion(s32[5120]{0:T(1024)} %get-tuple-element.227, f32[5120,1024]{1,0:T(8,128)} %bitcast.288, f32[]{:T(128)} %constant.63.clone.1), kind=kCustom, calls=%fused_computation.120 | custom fusion | flops 5242880 | bytes 2101760 | tf_op jit(solution)/shard_map/scatter-add | solution.py:157
  744.3 148.9 %while.29 = (s32[]{:T(128)}, f32[8,512,2,64]{1,3,2,0:T(8,128)S(1)}, bf16[8,2048,64]{1,2,0:T(8,128)(2,1)}, bf16[8,2048,64]{1,2,0:T(8,128)(2,1)}, bf16[8,2048,64]{...) while((s32[]{:T(128)}, f32[8,512,2,64]{1,3,2,0:T(8,128)S(1)}, ...), condition=%wide.region_21.22_spmd.clone, body=%wide.region_19.21_spmd.clone.sunk | while | flops 1376975872 | bytes 69776520 | solution.py:254
  893.3 4.7 pad_maximum_fusion.3
  901.7 39.3 %reduce-scatter.12.cloned.1.call-done = bf16[512,1024]{0,1:T(8,128)(2,1)} async-done(((bf16[2048,1024]{0,1:T(8,128)(2,1)}), bf16[512,1024]{0,1:T(8,128)(2,1)}) %reduce-scatter.12.cloned.1.call-update) | async-done | bytes 1048592 | tf_op jit(solution)/shard_map/reduce_scatter | solution.py:264
  954.1 7.3 fusion.89
  961.4 23.0 fusion.69
  984.5 32.7 fusion.67
  1017.2 60.2 %reduce-scatter.24.cloned.1.call-done = f32[32,16]{1,0:T(8,128)} async-done(((f32[1024,16]{1,0:T(8,128)}), f32[32,16]{1,0:T(8,128)}) %reduce-scatter.24.cloned.1.call-update) | async-done | bytes 2064
  1082.2 127.7 %reduce-scatter.22.cloned.1.call-done = f32[32,2]{1,0:T(8,128)} async-done(((f32[1024,2]{1,0:T(8,128)}), f32[32,2]{1,0:T(8,128)}) %reduce-scatter.22.cloned.1.call-update) | async-done | bytes 272
  1211.2 141.6 %reduce-scatter.16.cloned.1.call-done = f32[1024,32]{0,1:T(8,128)} async-done(((f32[1024,1024]{0,1:T(8,128)}), f32[1024,32]{0,1:T(8,128)}) %reduce-scatter.16.cloned.1.call-update) | async-done | bytes 131088 | tf_op jit(solution)/shard_map/reduce_scatter | solution.py:291
  1352.8 184.5 %reduce-scatter.14.cloned.1.call-done = f32[1024,64]{0,1:T(8,128)} async-done(((f32[1024,2048]{0,1:T(8,128)}), f32[1024,64]{0,1:T(8,128)}) %reduce-scatter.14.cloned.1.call-update) | async-done | bytes 262160 | tf_op jit(solution)/shard_map/reduce_scatter | solution.py:290
  1537.3 708.8 %reduce-scatter.20.cloned.1.call-done = f32[16,512,32]{1,2,0:T(8,128)} async-done(((f32[16,512,1024]{1,2,0:T(8,128)}), f32[16,512,32]{1,2,0:T(8,128)}) %reduce-scatter.20.cloned.1.call-update) | async-done | bytes 1048592 | tf_op jit(solution)/shard_map/reduce_scatter | solution.py:297
  2246.1 1405.4 %reduce-scatter.18.cloned.1.call-done = f32[16,1024,32]{1,2,0:T(8,128)} async-done(((f32[16,1024,1024]{1,2,0:T(8,128)}), f32[16,1024,32]{1,2,0:T(8,128)}) %reduce-scatter.18.cloned.1.call-update) | async-done | bytes 2097168 | tf_op jit(solution)/shard_map/reduce_scatter | solution.py:296
  (288 shorter events, 300.9 us)
Async XLA Ops:
  7.2 74.2 %all-gather.8.cloned.1.call-start = ((), (), s32[]{:S(2)}) async-start(), calls=%async_computation.7 | async-start | bytes 4325376 | tf_op jit(solution)/shard_map/all_gather | solution.py:58
  7.9 204.7 %all-gather.10.cloned.1.call-start = ((), (), s32[]{:S(2)}) async-start(), calls=%async_computation.8 | async-start | bytes 5242880 | tf_op jit(solution)/shard_map/all_gather | solution.py:101
  79.8 6.5 copy-start.31
  80.4 5.9 copy-start.29
  81.4 130.8 %copy-start.11 = (f32[512,32]{0,1:T(8,128)}, f32[512,32]{0,1:T(8,128)S(1)}, u32[]{:S(2)}) copy-start(f32[512,32]{0,1:T(8,128)S(1)} %get-tuple-element.232) | copy-start | bytes 196612
  90.4 26.8 copy-start.33
  90.4 206.7 %all-gather.12.cloned.1.call-start = ((), (), s32[]{:S(2)}) async-start(), calls=%async_computation.9 | async-start | bytes 2162688 | tf_op jit(solution)/shard_map/all_gather | solution.py:59
  91.1 285.8 %all-gather.14.cloned.1.call-start = ((), (), s32[]{:S(2)}) async-start(), calls=%async_computation.10 | async-start | bytes 34603008 | tf_op jit(solution)/shard_map/all_gather | solution.py:64
  91.7 402.4 %all-gather.16.cloned.1.call-start = ((), (), s32[]{:S(2)}) async-start(), calls=%async_computation.11 | async-start | bytes 17301504 | tf_op jit(solution)/shard_map/all_gather | solution.py:65
  92.3 848.8 %reduce-scatter.12.cloned.1.call-start = ((), (), s32[]{:S(2)}) async-start(), calls=%async_computation.12 | async-start | bytes 5242880 | tf_op jit(solution)/shard_map/reduce_scatter | solution.py:264
  216.4 5.3 copy-start.14
  303.7 22.4 copy-start.21
  303.7 24.1 copy-start.23
  494.1 21.3 copy-start.28
  515.4 23.7 copy-start.26
  672.8 62.2 %copy-start.7 = (bf16[1,512,1024]{2,1,0:T(8,128)(2,1)S(1)}, bf16[1,512,1024]{2,1,0:T(8,128)(2,1)}, u32[]{:S(2)}) copy-start(bf16[1,512,1024]{2,1,0:T(8,128)(2,1)} %param.15) | copy-start | bytes 3145732
  735.0 5.3 copy-start.35
  740.3 4.0 copy-start.15
  740.3 4.0 copy-start.20
  740.3 4.0 copy-start.25
  898.0 179.3 %reduce-scatter.24.cloned.1.call-start = ((), (), s32[]{:S(2)}) async-start(), calls=%async_computation.18 | async-start | bytes 540672
  900.3 42.6 %copy-start.8 = (bf16[1,512,1024]{2,1,0:T(8,128)(2,1)S(1)}, bf16[1,512,1024]{2,1,0:T(8,128)(2,1)}, u32[]{:S(2)}) copy-start(bf16[1,512,1024]{2,1,0:T(8,128)(2,1)} %param.14) | copy-start | bytes 3145732
  900.3 42.6 %copy-start.30 = (f32[1,1024]{1,0:T(1,128)S(1)}, f32[1,1024]{1,0:T(1,128)}, u32[]{:S(2)}) copy-start(f32[1,1024]{1,0:T(1,128)} %copy-done.29) | copy-start | bytes 12292
  900.3 42.6 %copy-start.32 = (f32[512]{0:T(512)S(1)}, f32[512]{0:T(512)}, u32[]{:S(2)}) copy-start(f32[512]{0:T(512)} %copy-done.31) | copy-start | bytes 6148
  901.6 308.2 %reduce-scatter.22.cloned.1.call-start = ((), (), s32[]{:S(2)}) async-start(), calls=%async_computation.17 | async-start | bytes 540672
  942.4 5.7 copy-start.18
  942.8 5.3 copy-start.17
  944.2 5.3 copy-start.1
  949.2 403.6 %reduce-scatter.16.cloned.1.call-start = ((), (), s32[]{:S(2)}) async-start(), calls=%async_computation.14 | async-start | bytes 4325376 | tf_op jit(solution)/shard_map/reduce_scatter | solution.py:291
  954.0 583.3 %reduce-scatter.14.cloned.1.call-start = ((), (), s32[]{:S(2)}) async-start(), calls=%async_computation.13 | async-start | bytes 8650752 | tf_op jit(solution)/shard_map/reduce_scatter | solution.py:290
  961.4 1284.7 %reduce-scatter.20.cloned.1.call-start = ((), (), s32[]{:S(2)}) async-start(), calls=%async_computation.16 | async-start | bytes 34603008 | tf_op jit(solution)/shard_map/reduce_scatter | solution.py:297
  984.4 2667.1 %reduce-scatter.18.cloned.1.call-start = ((), (), s32[]{:S(2)}) async-start(), calls=%async_computation.15 | async-start | bytes 69206016 | tf_op jit(solution)/shard_map/reduce_scatter | solution.py:296
  (16 other events, 34.9 us)
Sparse Core Ops, SparseCore 0:
  11.0 64.8 all-gather.7
  90.5 30.7 all-gather.9
  124.2 56.7 all-gather.11
  183.9 192.9 all-gather.13
  379.8 114.1 all-gather.15
  898.2 42.8 reduce-scatter.11
  943.3 133.9 reduce-scatter.23
  1079.6 130.2 reduce-scatter.21
  1212.8 139.9 reduce-scatter.15
  1355.6 181.6 reduce-scatter.13
  1540.3 705.7 reduce-scatter.19
  2249.0 1402.4 reduce-scatter.17
where the time goes:
time: 3670 us; the launch traced here: 3660 us
  waiting for transfers between devices  2800 us (76%)
  matrix products  349 us (10%)
  other arithmetic  206 us (6%)
  local copies, waits for them, and re-layouts  154 us (4%)
  blocking collectives  134 us (4%)
    reduce_scatter x1, waiting for transfers between devices, per_device(): lax.psum_scatter(grad_gate_up_local, ('seq', 'dp'), scatter_dimension=2,...  1410 us
    reduce_scatter x1, waiting for transfers between devices, per_device(): lax.psum_scatter(grad_down_local, ('seq', 'dp'), scatter_dimension=2, til...  709 us
    unnamed x14, waiting for transfers between devices  190 us
    reduce_scatter x1, waiting for transfers between devices, per_device(): lax.psum_scatter(grad_qkv_local, ('seq', 'dp'), scatter_dimension=1, tile...  184 us
    reduce_scatter x1, waiting for transfers between devices, per_device(): lax.psum_scatter(grad_out_local, ('seq', 'dp'), scatter_dimension=1, tile...  142 us
    all_gather x1, waiting for transfers between devices, per_device(): lax.all_gather(w_down, ('seq', 'dp'), axis=2, tiled=True)  80.3 us
  transfers between devices with their start and end apart: 12, of which 9 were waited for; matrix products, arithmetic and copies ran while one was open for 8% of the time, Pallas kernels for 0%

commit v1 on v0

v1 whole, which is shorter than its diff:
```python
import functools

import jax
import jax.numpy as jnp
from jax import lax
from jax.sharding import PartitionSpec as P

HEADS = 16
KV_HEADS = 8
HEAD_DIM = 64
FF = 512
EXPERTS = 16


NORM_EPSILON = 1e-06
ROPE_THETA = 10000.0


def rms_scale(tensor):
    return lax.rsqrt(jnp.mean(tensor * tensor, axis=-1, keepdims=True) + NORM_EPSILON)


def rotate(tensor, positions, direction):
    half_dim = tensor.shape[-1] // 2
    frequency = ROPE_THETA ** (-jnp.arange(half_dim, dtype=jnp.float32) / half_dim)
    angles = positions.astype(jnp.float32)[:, None] * frequency[None, :]
    cosine = jnp.cos(angles)[:, None, :]
    sine_part = direction * jnp.sin(angles)[:, None, :]
    first_half = tensor[..., :half_dim]
    second_half = tensor[..., half_dim:]
    return jnp.concatenate(
        [
            first_half * cosine - second_half * sine_part,
            second_half * cosine + first_half * sine_part,
        ],
        axis=-1,
    )


def ring_sum(parts, axis, size, dtype):
    if size == 1:
        return parts[0].astype(jnp.float32)
    if size > 16:
        return lax.psum_scatter(parts.astype(dtype), axis, scatter_dimension=0).astype(jnp.float32)
    order = list(range(0, size, 2)) + list(range(size - 1 - size % 2, 0, -2))
    place_of = [0] * size
    for place, owner in enumerate(order):
        place_of[owner] = place
    place = jnp.asarray(place_of, jnp.int32)[lax.axis_index(axis)]
    owners = jnp.asarray(order, jnp.int32)
    ahead = [(order[i], order[(i + 1) % size]) for i in range(size)]
    back = [(after, before) for before, after in ahead]
    half = parts.shape[1] // 2

    def piece(where, first):
        owner = owners[lax.rem(where + 4 * size, size)]
        block = lax.dynamic_slice_in_dim(parts, owner, 1, 0)[0]
        return (block[:half] if first else block[half:]).astype(jnp.float32)

    up = piece(place - 1, True)
    down = piece(place + 1, False)
    for step in range(1, size):
        up = lax.ppermute(up.astype(dtype), axis, ahead)
        down = lax.ppermute(down.astype(dtype), axis, back)
        up = up.astype(jnp.float32) + piece(place - 1 - step, True)
        down = down.astype(jnp.float32) + piece(place + 1 + step, False)
    return jnp.concatenate([up, down], axis=0)


def seq_sum(parts, dtype):
    moved = lax.all_to_all(parts.astype(dtype), "seq", 0, 0, tiled=True)
    return jnp.sum(moved.astype(jnp.float32), axis=0)


def per_device(
    seq_size, dp_size, tokens, cotangent, segments, routes, w_qkv, w_out, norm_gains, router, w_gate_up, w_down
):
    bf16 = jnp.bfloat16
    devices = seq_size * dp_size
    own_experts = EXPERTS // seq_size
    width = w_qkv.shape[0]
    qkv_cols, out_cols, small_cols = w_qkv.shape[1], w_out.shape[1], router.shape[1]
    small_rows = 2 + EXPERTS
    dense_rows = qkv_cols + out_cols
    packed_rows = -(-(dense_rows + 1) // 32) * 32

    def pack(qkv_part, out_part, small_part):
        blocks = qkv_part.shape[0]
        flat = small_part.reshape(blocks, 1, small_rows * small_cols)
        flat = jnp.pad(
            flat,
            ((0, 0), (0, packed_rows - dense_rows - 1), (0, width - small_rows * small_cols)),
        )
        return jnp.concatenate([qkv_part, out_part, flat], axis=1)

    packed = pack(
        w_qkv.T[None], w_out.T[None], jnp.concatenate([norm_gains, router], axis=0)[None]
    )[0]
    packed_full = lax.all_gather(packed, ("seq", "dp"), axis=0, tiled=False)
    qkv_t = packed_full[:, :qkv_cols].reshape(devices * qkv_cols, width)
    out_t = packed_full[:, qkv_cols:dense_rows].reshape(devices * out_cols, width)
    small = (
        packed_full[:, dense_rows, : small_rows * small_cols]
        .reshape(devices, small_rows, small_cols)
        .transpose(1, 0, 2)
        .reshape(small_rows, devices * small_cols)
    )
    gain_rows, router_proj = small[:2], small[2:]

    def own_weights(weight):
        depth, columns = weight.shape[1], weight.shape[2]
        turned = weight.transpose(0, 2, 1).reshape(seq_size, own_experts, columns, depth)
        moved = lax.all_to_all(turned, "seq", 0, 0, tiled=True).transpose(1, 0, 2, 3)
        whole = lax.all_gather(moved, "dp", axis=2, tiled=True)
        return whole.reshape(own_experts, devices * columns, depth)

    gate_up_t = own_weights(w_gate_up)
    down_t = own_weights(w_down)
    routes_seq = lax.all_gather(routes[0], "seq", axis=0, tiled=True)
    dy_seq = lax.all_gather(cotangent[0], "seq", axis=0, tiled=True)
    norm_gain = gain_rows.astype(jnp.float32)
    inputs = tokens[0].astype(jnp.float32)
    row_count = inputs.shape[0]
    feature_count = inputs.shape[1]
    length = segments.shape[1]
    score_scale = HEAD_DIM ** (-0.5)
    query_width = HEADS * HEAD_DIM
    key_width = KV_HEADS * HEAD_DIM
    group_size = HEADS // KV_HEADS
    row_start = lax.axis_index("seq") * row_count
    own_index = row_start + jnp.arange(row_count, dtype=jnp.int32)
    segment_row = segments[0]
    own_segment = lax.dynamic_slice_in_dim(segment_row, row_start, row_count)
    rotary = own_index - own_segment
    key_index = jnp.arange(length, dtype=jnp.int32)
    key_mask = (key_index[None, :] <= own_index[:, None]) & (
        segment_row[None, :] == own_segment[:, None]
    )
    first_scale = rms_scale(inputs)
    first_normed = inputs * first_scale
    first_hidden = (first_normed * norm_gain[0]).astype(jnp.bfloat16)
    projected = lax.dot_general(
        first_hidden, qkv_t, (((1,), (1,)), ((), ())), preferred_element_type=jnp.float32
    )
    queries = rotate(
        projected[:, :query_width].reshape(row_count, HEADS, HEAD_DIM), rotary, 1.0
    ).astype(jnp.bfloat16)
    key_rows = rotate(
        projected[:, query_width : query_width + key_width].reshape(row_count, KV_HEADS, HEAD_DIM),
        rotary,
        1.0,
    ).astype(jnp.bfloat16)
    value_rows = projected[:, query_width + key_width :].astype(jnp.bfloat16)
    outgoing = jnp.concatenate([key_rows.reshape(row_count, key_width), value_rows], axis=1)
    sequence_kv = lax.all_gather(outgoing, "seq", axis=0, tiled=True)
    keys_all = sequence_kv[:, :key_width].reshape(length, KV_HEADS, HEAD_DIM).transpose(1, 0, 2)
    values_all = sequence_kv[:, key_width:].reshape(length, KV_HEADS, HEAD_DIM).transpose(1, 0, 2)
    query_heads = queries.reshape(row_count, KV_HEADS, group_size, HEAD_DIM).transpose(1, 0, 2, 3)

    def head_scores(query_group, key_head):
        scores = (
            jnp.einsum("qgd,kd->gqk", query_group, key_head, preferred_element_type=jnp.float32)
            * score_scale
        )
        return jnp.where(key_mask[None], scores, -1e30)

    def forward_head(operands):
        query_group, key_head, value_head = operands
        scores = head_scores(query_group, key_head)
        row_peak = jnp.max(scores, axis=-1, keepdims=True)
        shifted = jnp.exp(scores - row_peak)
        row_total = jnp.sum(shifted, axis=-1, keepdims=True)
        softmax_weights = (shifted / row_total).astype(jnp.bfloat16)
        attended_head = jnp.einsum(
            "gqk,kd->qgd", softmax_weights, value_head, preferred_element_type=jnp.float32
        )
        return (attended_head.astype(jnp.bfloat16), (row_peak + jnp.log(row_total))[..., 0])

    attended_heads, log_totals = lax.map(forward_head, (query_heads, keys_all, values_all))
    attended = attended_heads.transpose(1, 0, 2, 3).reshape(row_count, query_width)
    residual = inputs + lax.dot_general(
        attended, out_t, (((1,), (1,)), ((), ())), preferred_element_type=jnp.float32
    )
    second_scale = rms_scale(residual)
    second_normed = residual * second_scale
    second_hidden = (second_normed * norm_gain[1]).astype(jnp.bfloat16)
    first_expert = lax.axis_index("seq") * own_experts
    hidden_seq = lax.all_gather(second_hidden, "seq", axis=0, tiled=True)

    def dense_gates(hidden, route_rows):
        logits = lax.dot_general(
            hidden, router_proj, (((1,), (1,)), ((), ())), preferred_element_type=jnp.float32
        )
        used = jnp.any(
            route_rows[:, :, None] == jnp.arange(EXPERTS, dtype=jnp.int32)[None, None, :], axis=1
        )
        kept = jnp.where(used, logits, -jnp.inf)
        shifted = jnp.exp(kept - jnp.max(kept, axis=-1, keepdims=True))
        return used, shifted / jnp.sum(shifted, axis=-1, keepdims=True)

    used, gates = dense_gates(second_hidden, routes[0])
    gates_seq = dense_gates(hidden_seq, routes_seq)[1]
    own_gates = lax.dynamic_slice_in_dim(gates_seq, first_expert, own_experts, 1)[:, :, None]
    inner = own_experts * FF
    gu = lax.dot_general(
        hidden_seq,
        gate_up_t.reshape(own_experts * 2 * FF, width),
        (((1,), (1,)), ((), ())),
        preferred_element_type=jnp.float32,
    ).reshape(length, own_experts, 2 * FF)
    gate_part = gu[..., :FF]
    up_part = gu[..., FF:]
    sigmoid_gate = jax.nn.sigmoid(gate_part)
    silu_gate = gate_part * sigmoid_gate
    act = (silu_gate * up_part).astype(bf16).astype(jnp.float32)
    act_gated = (act * own_gates).astype(bf16).reshape(length, inner)
    down_flat = down_t.transpose(1, 0, 2).reshape(width, inner)
    mixture_part = lax.dot_general(
        act_gated, down_flat, (((1,), (1,)), ((), ())), preferred_element_type=jnp.float32
    )
    grad_inner = jnp.dot(dy_seq, down_flat, preferred_element_type=jnp.float32).reshape(
        length, own_experts, FF
    )
    grad_gates_part = jnp.sum(act * grad_inner, axis=-1)
    grad_act = grad_inner * own_gates
    silu_slope = sigmoid_gate * (1.0 + gate_part * (1.0 - sigmoid_gate))
    grad_gu = (
        jnp.concatenate([grad_act * up_part * silu_slope, grad_act * silu_gate], axis=-1)
        .astype(bf16)
        .reshape(length, own_experts * 2 * FF)
    )
    grad_hidden_part = jnp.dot(
        grad_gu,
        gate_up_t.reshape(own_experts * 2 * FF, width),
        preferred_element_type=jnp.float32,
    )
    high = grad_gates_part.astype(bf16)
    low = (grad_gates_part - high.astype(jnp.float32)).astype(bf16)
    extra = jnp.pad(jnp.concatenate([high, low], axis=1), ((0, 0), (0, 128 - 2 * own_experts)))
    payload = jnp.concatenate([grad_hidden_part.astype(bf16), extra], axis=1)
    moved = lax.all_to_all(
        payload.reshape(seq_size, row_count, width + 128), "seq", 0, 0, tiled=True
    )
    grad_second = jnp.sum(moved[:, :, :width].astype(jnp.float32), axis=0)
    parts = moved[:, :, width : width + 2 * own_experts].astype(jnp.float32)
    grad_gates = (
        (parts[..., :own_experts] + parts[..., own_experts:])
        .transpose(1, 0, 2)
        .reshape(row_count, EXPERTS)
    )
    grad_output = cotangent[0].astype(jnp.float32)
    grad_logits = jnp.where(
        used,
        gates * (grad_gates - jnp.sum(gates * grad_gates, axis=-1, keepdims=True)),
        0.0,
    ).astype(bf16)
    grad_second = grad_second + jnp.dot(
        grad_logits, router_proj, preferred_element_type=jnp.float32
    )
    mixture = seq_sum(mixture_part.reshape(seq_size, row_count, width), bf16)
    mixed = (residual + mixture).astype(bf16)[None]

    def expert_owned(local):
        columns, depth = local.shape[1] // devices, local.shape[2]
        blocks = (
            local.astype(bf16)
            .reshape(own_experts, seq_size, dp_size, columns, depth)
            .transpose(2, 1, 0, 3, 4)
            .reshape(dp_size, seq_size * own_experts, columns, depth)
        )
        mine = ring_sum(blocks, "dp", dp_size, bf16)
        mine = mine.reshape(seq_size, own_experts, columns, depth)
        sent = lax.all_to_all(mine.astype(bf16), "seq", 0, 0, tiled=True)
        return (
            sent.reshape(EXPERTS, columns, depth).transpose(0, 2, 1).astype(jnp.float32)
        )

    grad_gate_up_local = lax.dot_general(
        grad_gu, hidden_seq, (((0,), (0,)), ((), ())), preferred_element_type=jnp.float32
    ).reshape(own_experts, 2 * FF, width)
    grad_gate_up = expert_owned(grad_gate_up_local)
    grad_down_local = (
        lax.dot_general(
            dy_seq, act_gated, (((0,), (0,)), ((), ())), preferred_element_type=jnp.float32
        )
        .astype(bf16)
        .reshape(width, own_experts, FF)
        .transpose(1, 0, 2)
    )
    grad_down = expert_owned(grad_down_local)
    grad_router_local = lax.dot_general(
        grad_logits, second_hidden, (((0,), (0,)), ((), ())), preferred_element_type=jnp.float32
    )
    gain_two = jnp.sum(grad_second * second_normed, axis=0)
    grad_normed_two = grad_second * norm_gain[1]
    grad_residual = grad_output + second_scale * (
        grad_normed_two
        - second_normed * jnp.mean(grad_normed_two * second_normed, axis=-1, keepdims=True)
    )
    grad_branch = grad_residual.astype(jnp.bfloat16)
    grad_attended = lax.dot_general(
        grad_branch, out_t, (((1,), (0,)), ((), ())), preferred_element_type=jnp.float32
    ).astype(jnp.bfloat16)
    grad_out_local = lax.dot_general(
        grad_branch, attended, (((0,), (0,)), ((), ())), preferred_element_type=jnp.float32
    )
    grad_heads = grad_attended.reshape(row_count, KV_HEADS, group_size, HEAD_DIM).transpose(
        1, 0, 2, 3
    )

    def backward_head(operands):
        query_group, key_head, value_head, grad_group, log_total = operands
        scores = head_scores(query_group, key_head)
        softmax_full = jnp.exp(scores - log_total[..., None])
        grad_weights = jnp.einsum(
            "qgd,kd->gqk", grad_group, value_head, preferred_element_type=jnp.float32
        )
        row_delta = jnp.sum(softmax_full * grad_weights, axis=-1, keepdims=True)
        grad_scores = (softmax_full * (grad_weights - row_delta)).astype(jnp.bfloat16)
        grad_query = (
            jnp.einsum("gqk,kd->qgd", grad_scores, key_head, preferred_element_type=jnp.float32)
            * score_scale
        )
        grad_key = (
            jnp.einsum("gqk,qgd->kd", grad_scores, query_group, preferred_element_type=jnp.float32)
            * score_scale
        )
        grad_value = jnp.einsum(
            "gqk,qgd->kd",
            softmax_full.astype(jnp.bfloat16),
            grad_group,
            preferred_element_type=jnp.float32,
        )
        return (grad_query, grad_key, grad_value)

    query_grads, key_grads, value_grads = lax.map(
        backward_head, (query_heads, keys_all, values_all, grad_heads, log_totals)
    )
    key_terms = jnp.concatenate(
        [
            key_grads.transpose(1, 0, 2).reshape(length, key_width),
            value_grads.transpose(1, 0, 2).reshape(length, key_width),
        ],
        axis=1,
    )
    key_owned = seq_sum(key_terms.reshape(seq_size, row_count, 2 * key_width), bf16)
    grad_query_rows = rotate(
        query_grads.transpose(1, 0, 2, 3).reshape(row_count, HEADS, HEAD_DIM), rotary, -1.0
    ).reshape(row_count, query_width)
    grad_key_rows = rotate(
        key_owned[:, :key_width].reshape(row_count, KV_HEADS, HEAD_DIM), rotary, -1.0
    ).reshape(row_count, key_width)
    grad_projected = jnp.concatenate(
        [grad_query_rows, grad_key_rows, key_owned[:, key_width:]], axis=1
    ).astype(jnp.bfloat16)
    grad_first = lax.dot_general(
        grad_projected, qkv_t, (((1,), (0,)), ((), ())), preferred_element_type=jnp.float32
    )
    grad_qkv_local = lax.dot_general(
        grad_projected, first_hidden, (((0,), (0,)), ((), ())), preferred_element_type=jnp.float32
    )
    gain_one = jnp.sum(grad_first * first_normed, axis=0)
    grad_normed_one = grad_first * norm_gain[0]
    input_grad = grad_residual + first_scale * (
        grad_normed_one
        - first_normed * jnp.mean(grad_normed_one * first_normed, axis=-1, keepdims=True)
    )
    small_grads = (
        jnp.concatenate([gain_one[None], gain_two[None], grad_router_local], axis=0)
        .reshape(small_rows, devices, small_cols)
        .transpose(1, 0, 2)
    )
    dense_grads = pack(
        grad_qkv_local.astype(bf16).reshape(devices, qkv_cols, width),
        grad_out_local.astype(bf16).reshape(devices, out_cols, width),
        small_grads.astype(bf16),
    ).reshape(seq_size, dp_size, packed_rows, width)
    dense_owned = ring_sum(seq_sum(dense_grads, bf16), "dp", dp_size, bf16)
    small_owned = dense_owned[dense_rows, : small_rows * small_cols].reshape(
        small_rows, small_cols
    )
    return (
        mixed,
        input_grad[None],
        dense_owned[:qkv_cols].T,
        dense_owned[qkv_cols:dense_rows].T,
        small_owned[:2],
        small_owned[2:],
        grad_gate_up,
        grad_down,
    )


def solution(mesh):
    placed = (
        P("dp", "seq", None),
        P("dp", "seq", None),
        P("dp", None),
        P("dp", "seq", None),
        P(None, ("seq", "dp")),
        P(None, ("seq", "dp")),
        P(None, ("seq", "dp")),
        P(None, ("seq", "dp")),
        P(None, None, ("seq", "dp")),
        P(None, None, ("seq", "dp")),
    )
    return jax.shard_map(
        functools.partial(per_device, mesh.shape["seq"], mesh.shape["dp"]),
        mesh=mesh,
        in_specs=placed,
        out_specs=(
            P("dp", "seq", None),
            P("dp", "seq", None),
            P(None, ("seq", "dp")),
            P(None, ("seq", "dp")),
            P(None, ("seq", "dp")),
            P(None, ("seq", "dp")),
            P(None, None, ("seq", "dp")),
            P(None, None, ("seq", "dp")),
        ),
        check_vma=False,
    )
```

time: 3670 us -> 1110 us (0.30)
  waiting for transfers between devices: 2800 us -> 310 us
  blocking collectives: 134 us -> 31 us
  starting transfers between devices: 0.74 us -> 75.4 us
  between operations: 15.3 us -> 55.6 us
    reduce_scatter x5 -> x0, waiting for transfers between devices: 2480 us -> none  [the longest x1 1410 us: per_device(): lax.psum_scatter(grad_gate_up_local, ('seq', 'dp'), scatter_dimension=2,...]
    unnamed x14 -> x6, waiting for transfers between devices: 190 us -> 0.6 us
    all_gather x2 -> x1, blocking collectives: 134 us -> 5.9 us  [per_device(): routes_seq = lax.all_gather(routes[0], 'seq', axis=0, tiled=True)]
    gather x4 -> x0, local copies, waits for them, and re-layouts: 97.2 us -> none  [the longest x1 28.7 us: per_device(): slot_gates = gate_flat[slot_table].reshape(EXPERTS, CAP, 1)]
    scatter-add x2 -> x0, other arithmetic: 93 us -> none  [the longest x1 46.6 us: per_device(): jax.ops.segment_sum(grad_expert_in.reshape(EXPERTS * CAP, feature_count),...]
    all_gather x4 -> x5, waiting for transfers between devices: 129 us -> 194 us  [the longest x2 107 us: own_weights(): whole = lax.all_gather(moved, 'dp', axis=2, tiled=True)]
    all_to_all x0 -> x7, waiting for transfers between devices: none -> 56.1 us  [the longest x1 33 us: per_device(): lax.all_to_all(payload.reshape(seq_size, row_count, width + 128), 'seq',...]
    ppermute x0 -> x42, waiting for transfers between devices: none -> 50.7 us  [the longest x21 35 us: ring_sum(): up = lax.ppermute(up.astype(dtype), axis, ahead)]
  transfers between devices with their start and end apart: 12 -> 55, of which waited for: 9 -> 30; matrix products, arithmetic and copies ran while one was open for 8% -> 30% of each run, Pallas kernels for 0% -> 0%
where the time goes in v1:
time: 1110 us
  matrix products  315 us (28%)
  waiting for transfers between devices  310 us (28%)
  other arithmetic  189 us (17%)
  local copies, waits for them, and re-layouts  130 us (12%)
  starting transfers between devices  75.4 us (7%)
  between operations  55.6 us (5%)
  blocking collectives  31 us (3%)
    all_gather x2, waiting for transfers between devices, own_weights(): whole = lax.all_gather(moved, 'dp', axis=2, tiled=True)  107 us
    all_gather x1, waiting for transfers between devices, per_device(): packed_full = lax.all_gather(packed, ('seq', 'dp'), axis=0, tiled=False)  78.8 us
    ppermute x21, waiting for transfers between devices, ring_sum(): up = lax.ppermute(up.astype(dtype), axis, ahead)  35 us
    all_to_all x1, waiting for transfers between devices, per_device(): lax.all_to_all(payload.reshape(seq_size, row_count, width + 128), 'seq',...  33 us
    dot_general x16, matrix products, head_scores(): jnp.einsum('qgd,kd->gqk', query_group, key_head, preferred_element_type=j...  32.8 us
    dot_general x8, matrix products, backward_head(): jnp.einsum('qgd,kd->gqk', grad_group, value_head, preferred_element_type=...  31.6 us
    dot_general x8, matrix products, forward_head(): jnp.einsum('gqk,kd->qgd', softmax_weights, value_head, preferred_element_...  31.5 us
    dot_general x1, matrix products, per_device(): jnp.dot(dy_seq, down_flat, preferred_element_type=jnp.float32)  27.9 us
  transfers between devices with their start and end apart: 55, of which 30 were waited for; matrix products, arithmetic and copies ran while one was open for 30% of the time, Pallas kernels for 0%

profile of v1, /device:TPU:0, one launch (start us, length us, event | category | flops | bytes accessed | tf_op | source)
XLA Modules:
  0.0 1106.0 jit_solution(13084418854598624900)
XLA Ops:
  12.9 78.8 %all-gather.9.cloned.1.call-done = bf16[32,128,1024]{2,1,0:T(8,128)(2,1)} async-done(((bf16[1,128,1024]{2,1,0:T(8,128)(2,1)}), bf16[32,128,1024]{2,1,0:T(8,128)(2,1)}) %all-gather.9.cloned.1.call-update) | async-done | bytes 8388624 | tf_op jit(solution)/shard_map/all_gather | solution.py:99
  106.2 12.3 %all-to-all-done.1 = bf16[4,4,32,512]{3,2,1,0:T(8,128)(2,1)S(1)} async-done(((bf16[4,4,32,512]{3,2,1,0:T(8,128)(2,1)}), bf16[4,4,32,512]{3,2,1,0:T(8,128)(2,1)S(1)}, u32[]{:S(2)}, u32[]{:S(2)}) %all-to-all-start.1) | async-done | bytes 524320 | tf_op jit(solution)/shard_map/all_to_all | solution.py:113
  130.6 8.4 all-gather.11.cloned.1.call-done
  148.2 75.1 %while.28 = (s32[]{:T(128)}, bf16[8,512,2,64]{1,3,2,0:T(8,128)(2,1)}, f32[8,2,512]{2,1,0:T(2,128)}, bf16[8,2048,64]{1,2,0:T(8,128)(2,1)}, bf16[8,2048,64]{1,2,0:...) while((s32[]{:T(128)}, ...), condition=%wide.region_4.5_spmd.clone, body=%wide.region_1.4_spmd.clone.sunk | while | flops 565246976 | bytes 30194276 | solution.py:179
  230.7 25.1 %all_to_all.40 = bf16[4,4,32,1024]{3,2,1,0:T(8,128)(2,1)S(1)} all-to-all(bf16[4,4,32,1024]{3,2,1,0:T(8,128)(2,1)S(1)} %bitcast.683), channel_id=1, replica_groups=mesh['seq'=4,'dp'=8] {'seq'}, dimensions={0} | all-to-all | bytes 2097152 | tf_op jit(solution)/shard_map/all_to_all | solution.py:113
  257.5 5.9 all-gather
  263.6 5.4 copy.156
  272.5 7.0 copy.175
  279.4 7.9 reshape.603
  291.2 106.9 %all-gather.15.cloned.1.call-done = bf16[4,4,256,1024]{3,2,1,0:T(8,128)(2,1)} async-done(((bf16[4,4,32,1024]{3,2,1,0:T(8,128)(2,1)}), bf16[4,4,256,1024]{3,2,1,0:T(8,128)(2,1)}) %all-gather.15.cloned.1.call-update) | async-done | bytes 8388624 | tf_op jit(solution)/shard_map/all_gather | solution.py:114
  398.1 25.5 %fusion.81 = f32[2048,4,1024]{0,2,1:T(8,128)} fusion(bf16[4,1024,1024]{2,1,0:T(8,128)(2,1)} %bitcast.699, bf16[2048,1024]{1,0:T(8,128)(2,1)} %all-gather.13.cloned.1.call-done), kind=kOutput, calls=%fused_computation.99 | convolution fusion | flops 17179869184 | bytes 46137344 | tf_op jit(solution)/shard_map/dot_general | solution.py:205
  423.6 8.6 all-gather.19.cloned.1.call-done
  432.2 27.9 %fusion.67 = (f32[2048,4]{0,1:T(4,128)S(1)}, bf16[2048,4,512]{0,2,1:T(8,128)(2,1)}, f32[2048,4,512]{0,2,1:T(8,128)}) fusion(f32[2048,4,1024]{0,2,1:T(8,128)} %fusion.81, bf16[4,512,1024]{2,1,0:T(8,128)(2,1)} %bitcast.666, bf16[1,2048,1024]{2,1,0:T(8,128)(2,1)} %all-gather.19.cloned.1.call-done), kind=kOutput, calls=%fused_computation.75 | convolution fusion | flops 8627675136 | bytes 67141632 | tf_op jit(solution)/shard_map/dot_general | solution.py:221
  460.1 9.8 fusion.66
  469.9 23.7 %multiply_multiply_fusion = (bf16[2048,4,512]{0,2,1:T(8,128)(2,1)}, bf16[2048,4,512]{0,2,1:T(8,128)(2,1)}) fusion(f32[2048,4,1024]{0,2,1:T(8,128)} %fusion.81, f32[2048,4,512]{0,2,1:T(8,128)} %get-tuple-element.298, f32[2048,4]{0,1:T(4,128)S(1)} %dynamic-slice_divide_fusion), kind=kLoop, calls=%fused_computation.79 | loop fusion | flops 58720256 | bytes 67141632 | tf_op jit(solution)/shard_map/mul | solution.py:228
  493.7 14.4 %dot_general.86 = bf16[4,512,2048]{1,0,2:T(4,128)(2,1)} reshape(bf16[2048,4,512]{0,2,1:T(8,128)(2,1)} %fusion.66) | data formatting | bytes 16777216 | tf_op jit(solution)/shard_map/dot_general | solution.py:218
  508.1 14.0 %fusion.86 = bf16[4,512,1024]{2,1,0:T(8,128)(2,1)} fusion(bf16[1024,2048,1]{1,0,2:T(8,128)(2,1)} %reshape.603, bf16[4,512,2048]{1,0,2:T(4,128)(2,1)} %dot_general.86), kind=kOutput, calls=%fused_computation.104 | convolution fusion | flops 8592031744 | bytes 16777216 | tf_op jit(solution)/shard_map/dot_general | solution.py:218
  527.1 8.1 maximum_convert_fusion
  535.3 5.8 copy-done.4
  541.1 21.2 %convolution_convert_fusion = bf16[2048,1024]{0,1:T(8,128)(2,1)} fusion(bf16[2048,4096]{0,1:T(8,128)(2,1)S(1)} %bitcast.657, bf16[4096,1024]{1,0:T(8,128)(2,1)} %bitcast.700), kind=kOutput, calls=%fused_computation.101 | convolution fusion | flops 17181966336 | bytes 29360128 | tf_op jit(solution)/shard_map/dot_general | solution.py:232
  567.6 7.8 all-to-all-done.2
  601.3 33.0 %all-to-all-done.3 = bf16[4,512,1152]{1,2,0:T(8,128)(2,1)} async-done(((bf16[4,512,1152]{1,2,0:T(8,128)(2,1)}), bf16[4,512,1152]{1,2,0:T(8,128)(2,1)}, u32[]{:S(2)}, u32[]{:S(2)}) %all-to-all-start.3) | async-done | bytes 4718624 | tf_op jit(solution)/shard_map/all_to_all | solution.py:241
  652.6 149.4 %while.29 = (s32[]{:T(128)}, f32[8,512,2,64]{1,3,2,0:T(8,128)S(1)}, bf16[8,2048,64]{1,2,0:T(8,128)(2,1)}, bf16[8,2048,64]{1,2,0:T(8,128)(2,1)}, bf16[8,2048,64]{...) while((s32[]{:T(128)}, f32[8,512,2,64]{1,3,2,0:T(8,128)S(1)}, ...), condition=%wide.region_19.20_spmd.clone, body=%wide.region_17.19_spmd.clone.sunk | while | flops 1376975872 | bytes 69776512 | solution.py:336
  823.2 23.6 %fusion.73 = bf16[4,1024,1024]{2,1,0:T(8,128)(2,1)} fusion(bf16[2048,4,1024]{0,2,1:T(8,128)(2,1)} %copy-done.4, bf16[2048,1024]{1,0:T(8,128)(2,1)} %all-gather.13.cloned.1.call-done), kind=kOutput, calls=%fused_computation.90 | convolution fusion | flops 17184063488 | bytes 29360128 | tf_op jit(solution)/shard_map/dot_general | solution.py:278
  846.8 8.6 copy.168
  862.5 8.6 collective-permute-done.14
  903.5 5.6 all-to-all-start.5
  921.6 13.9 %fusion.83 = bf16[2048,1024]{1,0:T(8,128)(2,1)} fusion(bf16[2048,2048]{0,1:T(8,128)(2,1)} %bitcast.646, bf16[1,2048,1024]{2,1,0:T(8,128)(2,1)} %all-gather.19.cloned.1.call-done), kind=kOutput, calls=%fused_computation.102 | convolution fusion | flops 8592031744 | bytes 16777216 | tf_op jit(solution)/shard_map/dot_general | solution.py:283
  935.4 6.2 copy.169
  961.5 7.9 collective-permute-done.29
  989.5 6.2 collective-permute-done.31
  1032.2 6.0 convert_reduce_fusion
  (451 shorter events, 505.6 us)
Async XLA Ops:
  7.2 84.5 %all-gather.9.cloned.1.call-start = ((), (), s32[]{:S(2)}) async-start(), calls=%async_computation.8 | async-start | bytes 8650752 | tf_op jit(solution)/shard_map/all_gather | solution.py:99
  9.7 129.3 %all-gather.11.cloned.1.call-start = ((), (), s32[]{:S(2)}) async-start(), calls=%async_computation.9 | async-start | bytes 5242880 | tf_op jit(solution)/shard_map/all_gather | solution.py:155
  102.6 15.9 %all-to-all-start.1 = ((bf16[4,4,32,512]{3,2,1,0:T(8,128)(2,1)}), bf16[4,4,32,512]{3,2,1,0:T(8,128)(2,1)S(1)}, u32[]{:S(2)}, u32[]{:S(2)}) async-start(bf16[4,4,32,512]{3,2,1,0:T(8,128)(2,1)} %bitcast.690), calls=%async_computation.1 | async-start | bytes 1048576 | tf_op jit(solution)/shard_map/all_to_all | solution.py:113
  106.1 157.4 %all-gather.17.cloned.1.call-start = ((), (), s32[]{:S(2)}) async-start(), calls=%async_computation.12 | async-start | bytes 4718592 | tf_op jit(solution)/shard_map/all_gather | solution.py:114
  119.3 168.4 %all-gather.13.cloned.1.call-start = ((), (), s32[]{:S(2)}) async-start(), calls=%async_computation.10 | async-start | bytes 5242880 | tf_op jit(solution)/shard_map/all_gather | solution.py:188
  230.7 167.4 %all-gather.15.cloned.1.call-start = ((), (), s32[]{:S(2)}) async-start(), calls=%async_computation.11 | async-start | bytes 9437184 | tf_op jit(solution)/shard_map/all_gather | solution.py:114
  256.9 175.3 %all-gather.19.cloned.1.call-start = ((), (), s32[]{:S(2)}) async-start(), calls=%async_computation.13 | async-start | bytes 5242880 | tf_op jit(solution)/shard_map/all_gather | solution.py:120
  522.1 53.3 %all-to-all-start.2 = ((bf16[4,512,1024]{2,1,0:T(8,128)(2,1)}), bf16[4,512,1024]{2,1,0:T(8,128)(2,1)}, u32[]{:S(2)}, u32[]{:S(2)}) async-start(bf16[4,512,1024]{2,1,0:T(8,128)(2,1)} %fusion.86), calls=%async_computation.2 | async-start | bytes 8388608 | tf_op jit(solution)/shard_map/all_to_all | solution.py:71
  575.3 58.9 %all-to-all-start.3 = ((bf16[4,512,1152]{1,2,0:T(8,128)(2,1)}), bf16[4,512,1152]{1,2,0:T(8,128)(2,1)}, u32[]{:S(2)}, u32[]{:S(2)}) async-start(bf16[4,512,1152]{1,2,0:T(8,128)(2,1)} %bitcast.647), calls=%async_computation.3 | async-start | bytes 9437184 | tf_op jit(solution)/shard_map/all_to_all | solution.py:241
  818.3 65.2 %all-to-all-start.4 = ((bf16[4,512,1024]{1,2,0:T(8,128)(2,1)}), bf16[4,512,1024]{1,2,0:T(8,128)(2,1)}, u32[]{:S(2)}, u32[]{:S(2)}) async-start(bf16[4,512,1024]{1,2,0:T(8,128)(2,1)} %copy.163), calls=%async_computation.4 | async-start | bytes 8388608 | tf_op jit(solution)/shard_map/all_to_all | solution.py:71
  856.8 14.3 %collective-permute-start.14 = (bf16[8,32,1024]{2,1,0:T(8,128)(2,1)S(1)}, bf16[8,32,1024]{2,1,0:T(8,128)(2,1)S(1)}, u32[]{:S(2)}, u32[]{:S(2)}) collective-permute-start(bf16[8,32,1024]{2,1,0:T(8,128)(2,1)S(1)} %get-tuple-element.231), channel_id=1, source_target_pairs={{0,2},{2,4},{4,6},{6,7},{7,5},{5,3},{3,1},{1,0},{8,10},{10,12},{12... | collective-permute-start | bytes 1572872 | tf_op jit(solution)/shard_map/ppermute | solution.py:63
  858.3 14.0 %collective-permute-start.21 = (bf16[8,32,1024]{2,1,0:T(8,128)(2,1)S(1)}, bf16[8,32,1024]{2,1,0:T(8,128)(2,1)S(1)}, u32[]{:S(2)}, u32[]{:S(2)}) collective-permute-start(bf16[8,32,1024]{2,1,0:T(8,128)(2,1)S(1)} %get-tuple-element.232), channel_id=1, source_target_pairs={{2,0},{4,2},{6,4},{7,6},{5,7},{3,5},{1,3},{0,1},{10,8},{12,10},{14... | collective-permute-start | bytes 1572872 | tf_op jit(solution)/shard_map/ppermute | solution.py:64
  874.9 41.5 %collective-permute-start.15 = (bf16[8,32,1024]{2,1,0:T(8,128)(2,1)}, bf16[8,32,1024]{2,1,0:T(8,128)(2,1)}, u32[]{:S(2)}, u32[]{:S(2)}) collective-permute-start(bf16[8,32,1024]{2,1,0:T(8,128)(2,1)} %get-tuple-element.229), channel_id=1, source_target_pairs={{0,2},{2,4},{4,6},{6,7},{7,5},{5,3},{3,1},{1,0},{8,10},{10,12},{12... | collective-permute-start | bytes 1572872 | tf_op jit(solution)/shard_map/ppermute | solution.py:63
  876.4 40.0 %collective-permute-start.22 = (bf16[8,32,1024]{2,1,0:T(8,128)(2,1)}, bf16[8,32,1024]{2,1,0:T(8,128)(2,1)}, u32[]{:S(2)}, u32[]{:S(2)}) collective-permute-start(bf16[8,32,1024]{2,1,0:T(8,128)(2,1)} %get-tuple-element.230), channel_id=1, source_target_pairs={{2,0},{4,2},{6,4},{7,6},{5,7},{3,5},{1,3},{0,1},{10,8},{12,10},{14... | collective-permute-start | bytes 1572872 | tf_op jit(solution)/shard_map/ppermute | solution.py:64
  903.5 128.7 %all-to-all-start.5 = ((bf16[4,8,128,1024]{3,2,1,0:T(8,128)(2,1)}), bf16[4,8,128,1024]{3,2,1,0:T(8,128)(2,1)}, u32[]{:S(2)}, u32[]{:S(2)}) async-start(bf16[4,8,128,1024]{3,2,1,0:T(8,128)(2,1)} %pad_maximum_fusion), calls=%async_computation.5 | async-start | bytes 16777216 | tf_op jit(solution)/shard_map/all_to_all | solution.py:71
  919.2 27.3 %collective-permute-start.16 = (bf16[8,32,1024]{2,1,0:T(8,128)(2,1)}, bf16[8,32,1024]{2,1,0:T(8,128)(2,1)S(1)}, u32[]{:S(2)}, u32[]{:S(2)}) collective-permute-start(bf16[8,32,1024]{2,1,0:T(8,128)(2,1)} %get-tuple-element.227), channel_id=1, source_target_pairs={{0,2},{2,4},{4,6},{6,7},{7,5},{5,3},{3,1},{1,0},{8,10},{10,12},{12... | collective-permute-start | bytes 1572872 | tf_op jit(solution)/shard_map/ppermute | solution.py:63
  920.6 25.8 %collective-permute-start.23 = (bf16[8,32,1024]{2,1,0:T(8,128)(2,1)S(1)}, bf16[8,32,1024]{2,1,0:T(8,128)(2,1)}, u32[]{:S(2)}, u32[]{:S(2)}) collective-permute-start(bf16[8,32,1024]{2,1,0:T(8,128)(2,1)S(1)} %get-tuple-element.228), channel_id=1, source_target_pairs={{2,0},{4,2},{6,4},{7,6},{5,7},{3,5},{1,3},{0,1},{10,8},{12,10},{14... | collective-permute-start | bytes 1572872 | tf_op jit(solution)/shard_map/ppermute | solution.py:64
  949.0 25.0 %collective-permute-start.17 = (bf16[8,32,1024]{2,1,0:T(8,128)(2,1)}, bf16[8,32,1024]{2,1,0:T(8,128)(2,1)S(1)}, u32[]{:S(2)}, u32[]{:S(2)}) collective-permute-start(bf16[8,32,1024]{2,1,0:T(8,128)(2,1)} %get-tuple-element.225), channel_id=1, source_target_pairs={{0,2},{2,4},{4,6},{6,7},{7,5},{5,3},{3,1},{1,0},{8,10},{10,12},{12... | collective-permute-start | bytes 1572872 | tf_op jit(solution)/shard_map/ppermute | solution.py:63
  950.5 23.5 %collective-permute-start.24 = (bf16[8,32,1024]{2,1,0:T(8,128)(2,1)S(1)}, bf16[8,32,1024]{2,1,0:T(8,128)(2,1)}, u32[]{:S(2)}, u32[]{:S(2)}) collective-permute-start(bf16[8,32,1024]{2,1,0:T(8,128)(2,1)S(1)} %get-tuple-element.226), channel_id=1, source_target_pairs={{2,0},{4,2},{6,4},{7,6},{5,7},{3,5},{1,3},{0,1},{10,8},{12,10},{14... | collective-permute-start | bytes 1572872 | tf_op jit(solution)/shard_map/ppermute | solution.py:64
  956.1 13.3 %collective-permute-start.29 = (bf16[8,32,512]{2,1,0:T(8,128)(2,1)}, bf16[8,32,512]{2,1,0:T(8,128)(2,1)S(1)}, u32[]{:S(2)}, u32[]{:S(2)}) collective-permute-start(bf16[8,32,512]{2,1,0:T(8,128)(2,1)} %get-tuple-element.245), channel_id=1, source_target_pairs={{0,2},{2,4},{4,6},{6,7},{7,5},{5,3},{3,1},{1,0},{8,10},{10,12},{12... | collective-permute-start | bytes 786440 | tf_op jit(solution)/shard_map/ppermute | solution.py:63
  957.5 13.1 %collective-permute-start.36 = (bf16[8,32,512]{2,1,0:T(8,128)(2,1)}, bf16[8,32,512]{2,1,0:T(8,128)(2,1)}, u32[]{:S(2)}, u32[]{:S(2)}) collective-permute-start(bf16[8,32,512]{2,1,0:T(8,128)(2,1)} %get-tuple-element.246), channel_id=1, source_target_pairs={{2,0},{4,2},{6,4},{7,6},{5,7},{3,5},{1,3},{0,1},{10,8},{12,10},{14... | collective-permute-start | bytes 786440 | tf_op jit(solution)/shard_map/ppermute | solution.py:64
  976.6 23.9 %collective-permute-start.18 = (bf16[8,32,1024]{2,1,0:T(8,128)(2,1)}, bf16[8,32,1024]{2,1,0:T(8,128)(2,1)S(1)}, u32[]{:S(2)}, u32[]{:S(2)}) collective-permute-start(bf16[8,32,1024]{2,1,0:T(8,128)(2,1)} %get-tuple-element.223), channel_id=1, source_target_pairs={{0,2},{2,4},{4,6},{6,7},{7,5},{5,3},{3,1},{1,0},{8,10},{10,12},{12... | collective-permute-start | bytes 1572872 | tf_op jit(solution)/shard_map/ppermute | solution.py:63
  978.1 22.4 %collective-permute-start.25 = (bf16[8,32,1024]{2,1,0:T(8,128)(2,1)S(1)}, bf16[8,32,1024]{2,1,0:T(8,128)(2,1)}, u32[]{:S(2)}, u32[]{:S(2)}) collective-permute-start(bf16[8,32,1024]{2,1,0:T(8,128)(2,1)S(1)} %get-tuple-element.224), channel_id=1, source_target_pairs={{2,0},{4,2},{6,4},{7,6},{5,7},{3,5},{1,3},{0,1},{10,8},{12,10},{14... | collective-permute-start | bytes 1572872 | tf_op jit(solution)/shard_map/ppermute | solution.py:64
  1003.0 24.4 %collective-permute-start.19 = (bf16[8,32,1024]{2,1,0:T(8,128)(2,1)}, bf16[8,32,1024]{2,1,0:T(8,128)(2,1)S(1)}, u32[]{:S(2)}, u32[]{:S(2)}) collective-permute-start(bf16[8,32,1024]{2,1,0:T(8,128)(2,1)} %get-tuple-element.221), channel_id=1, source_target_pairs={{0,2},{2,4},{4,6},{6,7},{7,5},{5,3},{3,1},{1,0},{8,10},{10,12},{12... | collective-permute-start | bytes 1572872 | tf_op jit(solution)/shard_map/ppermute | solution.py:63
  1004.5 23.0 %collective-permute-start.26 = (bf16[8,32,1024]{2,1,0:T(8,128)(2,1)S(1)}, bf16[8,32,1024]{2,1,0:T(8,128)(2,1)}, u32[]{:S(2)}, u32[]{:S(2)}) collective-permute-start(bf16[8,32,1024]{2,1,0:T(8,128)(2,1)S(1)} %get-tuple-element.222), channel_id=1, source_target_pairs={{2,0},{4,2},{6,4},{7,6},{5,7},{3,5},{1,3},{0,1},{10,8},{12,10},{14... | collective-permute-start | bytes 1572872 | tf_op jit(solution)/shard_map/ppermute | solution.py:64
  1010.5 12.8 %collective-permute-start.40 = (bf16[8,32,512]{2,1,0:T(8,128)(2,1)}, bf16[8,32,512]{2,1,0:T(8,128)(2,1)}, u32[]{:S(2)}, u32[]{:S(2)}) collective-permute-start(bf16[8,32,512]{2,1,0:T(8,128)(2,1)} %get-tuple-element.238), channel_id=1, source_target_pairs={{2,0},{4,2},{6,4},{7,6},{5,7},{3,5},{1,3},{0,1},{10,8},{12,10},{14... | collective-permute-start | bytes 786440 | tf_op jit(solution)/shard_map/ppermute | solution.py:64
  1025.4 16.2 %collective-permute-start.34 = (bf16[8,32,512]{2,1,0:T(8,128)(2,1)}, bf16[8,32,512]{2,1,0:T(8,128)(2,1)S(1)}, u32[]{:S(2)}, u32[]{:S(2)}) collective-permute-start(bf16[8,32,512]{2,1,0:T(8,128)(2,1)} %get-tuple-element.235), channel_id=1, source_target_pairs={{0,2},{2,4},{4,6},{6,7},{7,5},{5,3},{3,1},{1,0},{8,10},{10,12},{12... | collective-permute-start | bytes 786440 | tf_op jit(solution)/shard_map/ppermute | solution.py:63
  1026.0 17.2 %collective-permute-start.41 = (bf16[8,32,512]{2,1,0:T(8,128)(2,1)}, bf16[8,32,512]{2,1,0:T(8,128)(2,1)}, u32[]{:S(2)}, u32[]{:S(2)}) collective-permute-start(bf16[8,32,512]{2,1,0:T(8,128)(2,1)} %get-tuple-element.236), channel_id=1, source_target_pairs={{2,0},{4,2},{6,4},{7,6},{5,7},{3,5},{1,3},{0,1},{10,8},{12,10},{14... | collective-permute-start | bytes 786440 | tf_op jit(solution)/shard_map/ppermute | solution.py:64
  1030.2 21.9 %collective-permute-start.20 = (bf16[8,32,1024]{2,1,0:T(8,128)(2,1)}, bf16[8,32,1024]{2,1,0:T(8,128)(2,1)S(1)}, u32[]{:S(2)}, u32[]{:S(2)}) collective-permute-start(bf16[8,32,1024]{2,1,0:T(8,128)(2,1)} %get-tuple-element.219), channel_id=1, source_target_pairs={{0,2},{2,4},{4,6},{6,7},{7,5},{5,3},{3,1},{1,0},{8,10},{10,12},{12... | collective-permute-start | bytes 1572872 | tf_op jit(solution)/shard_map/ppermute | solution.py:63
  1030.8 22.1 %collective-permute-start.27 = (bf16[8,32,1024]{2,1,0:T(8,128)(2,1)}, bf16[8,32,1024]{2,1,0:T(8,128)(2,1)}, u32[]{:S(2)}, u32[]{:S(2)}) collective-permute-start(bf16[8,32,1024]{2,1,0:T(8,128)(2,1)} %get-tuple-element.220), channel_id=1, source_target_pairs={{2,0},{4,2},{6,4},{7,6},{5,7},{3,5},{1,3},{0,1},{10,8},{12,10},{14... | collective-permute-start | bytes 1572872 | tf_op jit(solution)/shard_map/ppermute | solution.py:64
  1045.3 15.1 %all-to-all-start.7 = ((bf16[4,4,32,512]{3,2,1,0:T(8,128)(2,1)}), bf16[4,4,32,512]{3,2,1,0:T(8,128)(2,1)S(1)}, u32[]{:S(2)}, u32[]{:S(2)}) async-start(bf16[4,4,32,512]{3,2,1,0:T(8,128)(2,1)} %bitcast.160), calls=%async_computation.7 | async-start | bytes 1048576 | tf_op jit(solution)/shard_map/all_to_all | solution.py:273
  1061.2 18.0 %all-to-all-start.6 = ((bf16[4,4,32,1024]{3,2,1,0:T(8,128)(2,1)}), bf16[4,4,32,1024]{3,2,1,0:T(8,128)(2,1)S(1)}, u32[]{:S(2)}, u32[]{:S(2)}) async-start(bf16[4,4,32,1024]{3,2,1,0:T(8,128)(2,1)} %bitcast.669), calls=%async_computation.6 | async-start | bytes 2097152 | tf_op jit(solution)/shard_map/all_to_all | solution.py:273
  (79 other events, 1019.4 us)
Sparse Core Ops, SparseCore 0:
  11.6 80.1 all-gather.8
  102.7 36.2 all-gather.10
  141.2 71.9 all-gather.16
  230.8 41.2 all-gather.12
  274.6 123.3 all-gather.14
  399.5 32.6 all-gather.18
